TPU v7x, 32 devices: a whole 2x2x4 slice. The times are simulated.
32 devices in a mesh: groups: 2 (over y), samples: 4 (over z), views: 2 (over x), rhs: 2 (over core).
Axes of the slice: x: 2, y: 2, z: 4, core: 2. Of those that a mesh axis runs over, the one named last changes fastest.
Arguments:
- features: bfloat16 [8, 8192, 128], P('views', ('groups', 'samples')), parts along dimension 1, may hold values from -8 to 8
- kernel_inverse_scale: float32 [8], replicated, may hold values from 0.0078125 to 0.0234375
- view_weight: float32 [8], replicated, may hold values from 0.05 to 0.3
- ridge_term: float32 [16], P('rhs'), may hold values from 0.5 to 4
- solution: float32 [8192, 16], P(('groups', 'samples'), 'rhs'), parts along dimension 0, may hold values from -6 to 6
- residual: float32 [8192, 16], P(('groups', 'samples'), 'rhs'), parts along dimension 0, may hold values from -210 to 210
- direction: float32 [8192, 16], P(('groups', 'samples'), 'rhs'), parts along dimension 0, may hold values from -210 to 210
Outputs:
- solution_next: float32 [8192, 16], P(('groups', 'samples'), 'rhs'), parts along dimension 0
- residual_next: float32 [8192, 16], P(('groups', 'samples'), 'rhs'), parts along dimension 0
- direction_next: float32 [8192, 16], P(('groups', 'samples'), 'rhs'), parts along dimension 0
There are 2 independent parts, one for each index of `groups`. A program takes and returns all parts, laid end to end along the dimension named above; an argument that names none is the same for every part. Nothing has to cross between parts.
All inputs are finite; a program needn't handle non-finite values.
Results may differ from a plain program's by a relative error of at most 0.0023.
Values may be sent and summed in bfloat16 or wider, within the bound.
A program may use at most 64 MiB of HBM per device.

v0:
```python
import jax
import jax.numpy as jnp
from jax import lax
from jax.sharding import PartitionSpec as P


def from_behind(value, axis, steps):
    count = lax.axis_size(axis)
    pairs = [(source, (source + steps) % count) for source in range(count)]
    return lax.ppermute(value, axis, pairs)


def per_device(
    features, kernel_inverse_scale, view_weight, ridge_term, solution, residual, direction
):
    local_views = features.shape[0]
    first_view = lax.axis_index("views") * local_views
    low_dir = direction.astype(jnp.bfloat16)
    scale_here = lax.dynamic_slice_in_dim(kernel_inverse_scale, first_view, local_views)
    weight_here = lax.dynamic_slice_in_dim(view_weight, first_view, local_views)
    row_norms = jnp.sum(jnp.square(features.astype(jnp.float32)), axis=-1)

    def tile_product(column_features, column_dir):
        column_sq_lengths = jnp.sum(jnp.square(column_features.astype(jnp.float32)), axis=-1)
        inner_rows = jnp.einsum(
            "snt,sgt->sng", features, column_features, preferred_element_type=jnp.float32
        )
        distance = row_norms[:, :, None] + column_sq_lengths[:, None, :] - 2.0 * inner_rows
        kernel = (
            weight_here[:, None, None] * jnp.exp(-scale_here[:, None, None] * distance)
        ).astype(jnp.bfloat16)
        return jnp.einsum("vij,jc->ic", kernel, column_dir, preferred_element_type=jnp.float32)

    running = tile_product(features, low_dir)
    period_length = lax.axis_size("samples")

    def one_turn(turn, carry):
        summed, moving_feats, moving_dir = carry
        moving_feats, moving_dir = from_behind((moving_feats, moving_dir), "samples", 1)
        return (summed + tile_product(moving_feats, moving_dir), moving_feats, moving_dir)

    running, _, _ = lax.fori_loop(0, period_length - 1, one_turn, (running, features, low_dir))
    summed_views = lax.psum(running, "views")
    product = summed_views + ridge_term[None, :] * direction
    norm_now, curvature = lax.psum(
        (jnp.sum(residual * residual, axis=0), jnp.sum(direction * product, axis=0)), "samples"
    )
    step_size = norm_now / curvature
    solution_next = solution + step_size * direction
    residual_next = residual - step_size * product
    norm_next = lax.psum(jnp.sum(residual_next * residual_next, axis=0), "samples")
    direction_next = residual_next + norm_next / norm_now * direction
    return (solution_next, residual_next, direction_next)


def solution(mesh):
    return jax.shard_map(
        per_device,
        mesh=mesh,
        in_specs=(
            P("views", ("groups", "samples"), None),
            P(),
            P(),
            P("rhs"),
            P(("groups", "samples"), "rhs"),
            P(("groups", "samples"), "rhs"),
            P(("groups", "samples"), "rhs"),
        ),
        out_specs=(
            P(("groups", "samples"), "rhs"),
            P(("groups", "samples"), "rhs"),
            P(("groups", "samples"), "rhs"),
        ),
        check_vma=False,
    )
```

profile of v0, /device:TPU:0, one launch (start us, length us, event | category | flops | bytes accessed | tf_op | source)
XLA Modules:
  0.0 143.5 jit_solution(14339561552583450636)
XLA Ops:
  0.6 0.7 dynamic_slice.6
  1.4 0.7 dynamic-slice_negate_fusion
  2.1 1.8 %multiply_reduce_fusion.1 = f32[4,1024]{1,0:T(4,128)S(1)} fusion(bf16[4,1024,128]{2,1,0:T(8,128)(2,1)} %param.9), kind=kLoop, calls=%fused_computation.6 | loop fusion | flops 1568768 | bytes 1064960 | tf_op jit(solution)/shard_map/reduce_sum | solution.py:21
  4.0 6.8 %convert_reduce_fusion.1 = bf16[1024,1024]{1,0:T(8,128)(2,1)S(1)} fusion(bf16[4,1024,128]{2,1,0:T(8,128)(2,1)} %param.9, f32[4,1024]{1,0:T(4,128)S(1)} %multiply_reduce_fusion.1, f32[4]{0:T(128)S(1)} %dynamic-slice_negate_fusion, f32[4]{0:T(128)S(1)} %dynamic_slice.6), kind=kOutput, calls=%fused_computation.4 | convolution fusion | flops 1106247680 | bytes 3162144 | tf_op jit(solution)/shard_map/snt,sgt->sng/dot_general | solution.py:25
  10.8 0.6 fusion
  12.1 102.9 %while.16 = (s32[]{:T(128)}, f32[1024,8]{0,1:T(8,128)S(1)}, bf16[4,1024,128]{2,1,0:T(8,128)(2,1)S(1)}, bf16[1024,8]{0,1:T(8,128)(2,1)S(1)}, f32[4]{0:T(128)S(1)}...) while((s32[]{:T(128)}, f32[1024,8]{0,1:T(8,128)S(1)}, ...), condition=%wide.region_7.0_spmd, body=%wide.region_4.7_spmd.sunk | while | flops 1124601856 | bytes 13861069 | solution.py:42
  12.1 3.1 %collective-permute-start = (bf16[4,1024,128]{2,1,0:T(8,128)(2,1)S(1)}, bf16[4,1024,128]{2,1,0:T(8,128)(2,1)S(1)}, u32[]{:S(2)}, u32[]{:S(2)}) collective-permute-start(bf16[4,1024,128]{2,1,0:T(8,128)(2,1)S(1)} %get-tuple-element.179), channel_id=1, source_target_pairs={{0,4},{4,8},{8,12},{12,0},{1,5},{5,9},{9,13},{13,1},{2,6},{6,10},{... | collective-permute-start | bytes 3145736 | tf_op jit(solution)/shard_map/while/body/eval_jaxpr/ppermute | solution.py:10
  15.2 1.6 %collective-permute-start.1 = (bf16[1024,8]{0,1:T(8,128)(2,1)S(1)}, bf16[1024,8]{0,1:T(8,128)(2,1)S(1)}, u32[]{:S(2)}, u32[]{:S(2)}) collective-permute-start(bf16[1024,8]{0,1:T(8,128)(2,1)S(1)} %get-tuple-element.180), channel_id=1, source_target_pairs={{0,4},{4,8},{8,12},{12,0},{1,5},{5,9},{9,13},{13,1},{2,6},{6,10},{... | collective-permute-start | bytes 49160 | tf_op jit(solution)/shard_map/while/body/eval_jaxpr/ppermute | solution.py:10
  16.8 23.9 %collective-permute-done.1 = bf16[1024,8]{0,1:T(8,128)(2,1)S(1)} collective-permute-done((bf16[1024,8]{0,1:T(8,128)(2,1)S(1)}, bf16[1024,8]{0,1:T(8,128)(2,1)S(1)}, u32[]{:S(2)}, u32[]{:S(2)}) %collective-permute-start.1) | collective-permute-done | bytes 16416 | tf_op jit(solution)/shard_map/while/body/eval_jaxpr/ppermute | solution.py:10
  40.7 0.6 multiply_reduce_fusion.6
  41.4 6.0 %convert_reduce_fusion.3 = bf16[1024,1024]{1,0:T(8,128)(2,1)S(1)} fusion(bf16[4,1024,128]{2,1,0:T(8,128)(2,1)S(1)} %get-tuple-element.193, bf16[4,1024,128]{2,1,0:T(8,128)(2,1)S(1)} %collective-permute-done, f32[4,1024]{1,0:T(4,128)S(1)} %multiply_reduce_fusion.6, f32[4,1024]{1,0:T(4,128)S(1)} %get-tuple-element.192, f32[4]{0:T(128)S(1)} %bitcast.21, ...), kind=kOutput, calls=%fused_computation.clone.1 | convolution fusion | flops 1106247680 | bytes 4227104 | tf_op jit(solution)/shard_map/while/body/eval_jaxpr/snt,sgt->sng/dot_general | solution.py:25
  47.5 0.6 convolution_add_fusion.2
  48.1 1.3 collective-permute-start.1
  49.4 25.2 %collective-permute-done.1 = bf16[1024,8]{0,1:T(8,128)(2,1)S(1)} collective-permute-done((bf16[1024,8]{0,1:T(8,128)(2,1)S(1)}, bf16[1024,8]{0,1:T(8,128)(2,1)S(1)}, u32[]{:S(2)}, u32[]{:S(2)}) %collective-permute-start.1) | collective-permute-done | bytes 16416 | tf_op jit(solution)/shard_map/while/body/eval_jaxpr/ppermute | solution.py:10
  75.3 6.0 %convert_reduce_fusion.3 = bf16[1024,1024]{1,0:T(8,128)(2,1)S(1)} fusion(bf16[4,1024,128]{2,1,0:T(8,128)(2,1)S(1)} %get-tuple-element.193, bf16[4,1024,128]{2,1,0:T(8,128)(2,1)S(1)} %collective-permute-done, f32[4,1024]{1,0:T(4,128)S(1)} %multiply_reduce_fusion.6, f32[4,1024]{1,0:T(4,128)S(1)} %get-tuple-element.192, f32[4]{0:T(128)S(1)} %bitcast.21, ...), kind=kOutput, calls=%fused_computation.clone.1 | convolution fusion | flops 1106247680 | bytes 4227104 | tf_op jit(solution)/shard_map/while/body/eval_jaxpr/snt,sgt->sng/dot_general | solution.py:25
  81.4 0.6 convolution_add_fusion.2
  82.1 25.5 %collective-permute-done.1 = bf16[1024,8]{0,1:T(8,128)(2,1)S(1)} collective-permute-done((bf16[1024,8]{0,1:T(8,128)(2,1)S(1)}, bf16[1024,8]{0,1:T(8,128)(2,1)S(1)}, u32[]{:S(2)}, u32[]{:S(2)}) %collective-permute-start.1) | collective-permute-done | bytes 16416 | tf_op jit(solution)/shard_map/while/body/eval_jaxpr/ppermute | solution.py:10
  108.3 6.0 %convert_reduce_fusion.3 = bf16[1024,1024]{1,0:T(8,128)(2,1)S(1)} fusion(bf16[4,1024,128]{2,1,0:T(8,128)(2,1)S(1)} %get-tuple-element.193, bf16[4,1024,128]{2,1,0:T(8,128)(2,1)S(1)} %collective-permute-done, f32[4,1024]{1,0:T(4,128)S(1)} %multiply_reduce_fusion.6, f32[4,1024]{1,0:T(4,128)S(1)} %get-tuple-element.192, f32[4]{0:T(128)S(1)} %bitcast.21, ...), kind=kOutput, calls=%fused_computation.clone.1 | convolution fusion | flops 1106247680 | bytes 4227104 | tf_op jit(solution)/shard_map/while/body/eval_jaxpr/snt,sgt->sng/dot_general | solution.py:25
  114.4 0.6 convolution_add_fusion.2
  115.0 7.9 %psum.29 = f32[1024,8]{0,1:T(8,128)S(1)} all-reduce(f32[1024,8]{0,1:T(8,128)S(1)} %get-tuple-element.97), channel_id=1, replica_groups=mesh['groups'=2,'samples'=4,'views'=2,'rhs'=2] {'views'}, use_global_device_ids=true, to_apply=%region_8.0 | all-reduce | flops 8192 | bytes 65536 | tf_op jit(solution)/shard_map/psum | solution.py:43
  123.2 8.4 %all-reduce = (f32[8]{0:T(128)S(1)}, f32[8]{0:T(128)S(1)}) all-reduce(f32[8]{0:T(128)S(1)} %multiply_reduce_fusion.4, f32[8]{0:T(128)S(1)} %multiply_reduce_fusion.3), channel_id=1, replica_groups=mesh['groups'=2,'samples'=4,'views'=2,'rhs'=2] {'samples'}, use_global_device_ids=true, to_apply=%region_1.0 | all-reduce | flops 16 | bytes 128 | tf_op jit(solution)/shard_map/psum | solution.py:45
  131.6 0.8 multiply_reduce_fusion.2
  132.4 10.4 %psum.31 = f32[8]{0:T(128)S(1)} all-reduce(f32[8]{0:T(128)S(1)} %get-tuple-element.116), channel_id=1, replica_groups=mesh['groups'=2,'samples'=4,'views'=2,'rhs'=2] {'samples'}, use_global_device_ids=true, to_apply=%region_12.0 | all-reduce | flops 8 | bytes 64 | tf_op jit(solution)/shard_map/psum | solution.py:51
  142.8 0.7 multiply_add_fusion
  (35 shorter events, 2.5 us)
Async XLA Ops:
  3.9 6.8 %copy-start.1 = (f32[1024,8]{0,1:T(8,128)S(1)}, f32[1024,8]{0,1:T(8,128)}, u32[]{:S(2)}) copy-start(f32[1024,8]{0,1:T(8,128)} %param.15) | copy-start | bytes 98308
  10.7 0.7 copy-start.6
  10.7 1.2 copy-start
  12.0 110.8 %copy-start.5 = (f32[8]{0:T(128)S(1)}, f32[8]{0:T(128)}, u32[]{:S(2)}) copy-start(f32[8]{0:T(128)} %param.12) | copy-start | bytes 100
  12.1 111.0 %copy-start.3 = (f32[1024,8]{0,1:T(8,128)S(1)}, f32[1024,8]{0,1:T(8,128)}, u32[]{:S(2)}) copy-start(f32[1024,8]{0,1:T(8,128)} %param.14) | copy-start | bytes 98308
  12.1 119.5 %copy-start.4 = (f32[1024,8]{0,1:T(8,128)S(1)}, f32[1024,8]{0,1:T(8,128)}, u32[]{:S(2)}) copy-start(f32[1024,8]{0,1:T(8,128)} %param.13) | copy-start | bytes 98308
  12.1 28.6 %collective-permute-start = (bf16[4,1024,128]{2,1,0:T(8,128)(2,1)S(1)}, bf16[4,1024,128]{2,1,0:T(8,128)(2,1)S(1)}, u32[]{:S(2)}, u32[]{:S(2)}) collective-permute-start(bf16[4,1024,128]{2,1,0:T(8,128)(2,1)S(1)} %get-tuple-element.179), channel_id=1, source_target_pairs={{0,4},{4,8},{8,12},{12,0},{1,5},{5,9},{9,13},{13,1},{2,6},{6,10},{... | collective-permute-start | bytes 3145736 | tf_op jit(solution)/shard_map/while/body/eval_jaxpr/ppermute | solution.py:10
  15.2 25.5 %collective-permute-start.1 = (bf16[1024,8]{0,1:T(8,128)(2,1)S(1)}, bf16[1024,8]{0,1:T(8,128)(2,1)S(1)}, u32[]{:S(2)}, u32[]{:S(2)}) collective-permute-start(bf16[1024,8]{0,1:T(8,128)(2,1)S(1)} %get-tuple-element.180), channel_id=1, source_target_pairs={{0,4},{4,8},{8,12},{12,0},{1,5},{5,9},{9,13},{13,1},{2,6},{6,10},{... | collective-permute-start | bytes 49160 | tf_op jit(solution)/shard_map/while/body/eval_jaxpr/ppermute | solution.py:10
  48.1 26.5 %collective-permute-start = (bf16[4,1024,128]{2,1,0:T(8,128)(2,1)S(1)}, bf16[4,1024,128]{2,1,0:T(8,128)(2,1)S(1)}, u32[]{:S(2)}, u32[]{:S(2)}) collective-permute-start(bf16[4,1024,128]{2,1,0:T(8,128)(2,1)S(1)} %get-tuple-element.179), channel_id=1, source_target_pairs={{0,4},{4,8},{8,12},{12,0},{1,5},{5,9},{9,13},{13,1},{2,6},{6,10},{... | collective-permute-start | bytes 3145736 | tf_op jit(solution)/shard_map/while/body/eval_jaxpr/ppermute | solution.py:10
  48.1 26.5 %collective-permute-start.1 = (bf16[1024,8]{0,1:T(8,128)(2,1)S(1)}, bf16[1024,8]{0,1:T(8,128)(2,1)S(1)}, u32[]{:S(2)}, u32[]{:S(2)}) collective-permute-start(bf16[1024,8]{0,1:T(8,128)(2,1)S(1)} %get-tuple-element.180), channel_id=1, source_target_pairs={{0,4},{4,8},{8,12},{12,0},{1,5},{5,9},{9,13},{13,1},{2,6},{6,10},{... | collective-permute-start | bytes 49160 | tf_op jit(solution)/shard_map/while/body/eval_jaxpr/ppermute | solution.py:10
  82.0 25.6 %collective-permute-start = (bf16[4,1024,128]{2,1,0:T(8,128)(2,1)S(1)}, bf16[4,1024,128]{2,1,0:T(8,128)(2,1)S(1)}, u32[]{:S(2)}, u32[]{:S(2)}) collective-permute-start(bf16[4,1024,128]{2,1,0:T(8,128)(2,1)S(1)} %get-tuple-element.179), channel_id=1, source_target_pairs={{0,4},{4,8},{8,12},{12,0},{1,5},{5,9},{9,13},{13,1},{2,6},{6,10},{... | collective-permute-start | bytes 3145736 | tf_op jit(solution)/shard_map/while/body/eval_jaxpr/ppermute | solution.py:10
  82.0 25.6 %collective-permute-start.1 = (bf16[1024,8]{0,1:T(8,128)(2,1)S(1)}, bf16[1024,8]{0,1:T(8,128)(2,1)S(1)}, u32[]{:S(2)}, u32[]{:S(2)}) collective-permute-start(bf16[1024,8]{0,1:T(8,128)(2,1)S(1)} %get-tuple-element.180), channel_id=1, source_target_pairs={{0,4},{4,8},{8,12},{12,0},{1,5},{5,9},{9,13},{13,1},{2,6},{6,10},{... | collective-permute-start | bytes 49160 | tf_op jit(solution)/shard_map/while/body/eval_jaxpr/ppermute | solution.py:10
  132.4 11.1 %copy-start.2 = (f32[1024,8]{0,1:T(8,128)}, f32[1024,8]{0,1:T(8,128)S(1)}, u32[]{:S(2)}) copy-start(f32[1024,8]{0,1:T(8,128)S(1)} %get-tuple-element.117) | copy-start | bytes 98308
where the time goes:
time: 144 us; the launch traced here: 143 us
  waiting for transfers between devices  74.7 us (52%)
  matrix products  27.4 us (19%)
  blocking collectives  26.6 us (18%)
  other arithmetic  6.36 us (4%)
  starting transfers between devices  6.01 us (4%)
  local copies, waits for them, and re-layouts  1.53 us (1%)
    ppermute x6, waiting for transfers between devices, from_behind(): return lax.ppermute(value, axis, pairs)  74.7 us
    dot_general x4, matrix products, tile_product(): jnp.einsum('snt,sgt->sng', features, column_features, preferred_element_t...  24.9 us
    psum x1, blocking collectives, per_device(): lax.psum(jnp.sum(residual_next * residual_next, axis=0), 'samples')  10.4 us
    psum x1, blocking collectives, per_device(): lax.psum((jnp.sum(residual * residual, axis=0), jnp.sum(direction * produ...  8.38 us
    psum x1, blocking collectives, per_device(): summed_views = lax.psum(running, 'views')  7.86 us
    ppermute x6, starting transfers between devices, from_behind(): return lax.ppermute(value, axis, pairs)  6.01 us
  transfers between devices with their start and end apart: 6, of which 3 were waited for; matrix products, arithmetic and copies ran while one was open for 0% of the time, Pallas kernels for 0%

commit v1 on v0

v1 whole, which is shorter than its diff:
```python
import functools
import math

import jax
import jax.numpy as jnp
from jax import lax
from jax.experimental import pallas as pl
from jax.experimental.pallas import tpu as pltpu
from jax.sharding import PartitionSpec as P

MESH = pl.DeviceIdType.MESH
LANES = (((1,), (1,)), ((), ()))


def cg_kernel(
    n, slots, tile,
    scale_ref, weight_ref, feats_ref, ridge_ref, sol_ref, res_ref, dir_ref,
    sol_out, res_out, dir_out,
    buf, dbuf, dpair, acc, ext_acc, norms, cout, cin, part, gath, stats,
    load_sem, fs, fr, ds, dr, ps, pr, cs, cr, es, er, gs, gr, ss, sr, dir_stage,
):
    z = lax.axis_index("samples")
    x = lax.axis_index("views")
    c = lax.axis_index("rhs")
    xs = lax.axis_size("views")
    local_views = feats_ref.shape[0]
    first_view = x * local_views
    rows = feats_ref.shape[1]
    half = local_views // 2

    if slots == 2:
        view = [c, half + c]
        sgn = [1, -1]
        pos = [z, n - 1 - z]
    else:
        view = [c]
        sgn = [1 - 2 * c]
        pos = [z * (1 - c) + (n - 1 - z) * c]

    def load(s):
        return pltpu.make_async_copy(feats_ref.at[view[s]], buf.at[s, 0], load_sem.at[s])

    for s in range(slots):
        load(s).start()

    barrier = pltpu.get_barrier_semaphore()
    peers = [{"samples": lax.rem(z + k, n)} for k in range(1, n)]
    cross = [(dx, dc) for dx in range(xs) for dc in range(2) if (dx, dc) != (0, 0)]
    peers += [{"views": lax.rem(x + dx, xs), "rhs": lax.rem(c + dc, 2)} for dx, dc in cross]
    for peer in peers:
        pl.semaphore_signal(barrier, inc=1, device_id=peer, device_id_type=MESH)
    pl.semaphore_wait(barrier, len(peers))

    def remote(src, dst, send, recv, target):
        return pltpu.make_async_remote_copy(
            src_ref=src, dst_ref=dst, send_sem=send, recv_sem=recv,
            device_id=target, device_id_type=MESH,
        )

    def ahead(s, steps):
        return {"samples": lax.rem(z + sgn[s] * steps + 2 * n, n)}

    def forward(s, d):
        return (
            remote(buf.at[s, d], buf.at[s, d + 1], fs.at[s, d], fr.at[s, d + 1], ahead(s, 1)),
            remote(dbuf.at[s, d], dbuf.at[s, d + 1], ds.at[s, d], dr.at[s, d + 1], ahead(s, 1)),
        )

    def back(s):
        return (
            remote(buf.at[s, 0], buf.at[s, n - 1], fs.at[s, n - 1], fr.at[s, n - 1], ahead(s, -1)),
            remote(dbuf.at[s, 0], dbuf.at[s, n - 1], ds.at[s, n - 1], dr.at[s, n - 1], ahead(s, -1)),
        )

    def give(s, d):
        return remote(cout.at[s, d], cin.at[s, d], cs.at[s, d], cr.at[s, d], ahead(s, -d))

    def give_end(s):
        return remote(ext_acc.at[s], cin.at[s, n - 1], es.at[s], cr.at[s, n - 1], ahead(s, 1))

    pair = remote(dir_ref, dpair.at[c], ps, pr, {"rhs": 1 - c})
    pair.start()
    stage = pltpu.make_async_copy(dir_ref, dpair.at[c], dir_stage)
    stage.start()
    for s in range(slots):
        load(s).wait()

        @pl.when(pos[s] < n - 1)
        def _(s=s):
            forward(s, 0)[0].start()

    stage.wait()
    pair.wait()
    low = jnp.concatenate([dpair[0], dpair[1]], axis=0).astype(jnp.bfloat16)
    for s in range(slots):
        dbuf[s, 0] = low

        @pl.when(pos[s] < n - 1)
        def _(s=s):
            forward(s, 0)[1].start()

    def consts(s):
        index = first_view + view[s]
        rate = scale_ref[index] * math.log2(math.e)
        return rate, jnp.log2(jnp.full((1, 1), weight_ref[index], jnp.float32))

    def row_term(s, slot_ref):
        rate, low_weight = consts(s)
        feats = slot_ref[...].astype(jnp.float32)
        sums = lax.dot_general(
            jnp.ones((8, feats.shape[1]), jnp.float32), feats * feats, LANES,
            precision=lax.Precision.HIGHEST, preferred_element_type=jnp.float32,
        )
        norms[s] = low_weight - rate * sums

    def block(s, jb, ib, jd, i_sum, j_sum, add_j):
        rate, _ = consts(s)

        def step(t, _):
            at = pl.ds(pl.multiple_of(t * tile, tile), tile)
            fj = jb[at, :]
            inner = lax.dot_general(fj, ib[...], LANES, preferred_element_type=jnp.float32)
            wide = fj.astype(jnp.float32)
            column = -rate * jnp.sum(wide * wide, axis=-1, keepdims=True)
            power = (2.0 * rate) * inner + norms[s, 0:1, :] + column
            kern = jnp.exp2(power).astype(jnp.bfloat16)
            i_sum[...] += jnp.dot(jd[:, at], kern, preferred_element_type=jnp.float32)
            if j_sum is not None:
                (idir, target) = j_sum
                term = lax.dot_general(idir[...], kern, LANES, preferred_element_type=jnp.float32)
                if add_j:
                    target[:, at] += term
                else:
                    target[:, at] = term
            return 0

        lax.fori_loop(0, rows // tile, step, 0)

    acc[...] = jnp.zeros_like(acc)
    for s in range(slots):
        row_term(s, buf.at[s, 0])
        block(s, buf.at[s, 0], buf.at[s, 0], dbuf.at[s, 0], acc, None, False)

    for s in range(slots):
        @pl.when(pos[s] == n - 1)
        def _(s=s):
            if slots == 2:
                forward(1 - s, 0)[0].wait_send()
            for copy in back(s):
                copy.start()

    def turn(d, _):
        for s in range(slots):
            @pl.when(pos[s] >= d)
            def _(s=s):
                for copy in forward(s, d - 1):
                    copy.wait_recv()

                @pl.when((pos[s] < n - 1) & (d < n - 2))
                def _():
                    for copy in forward(s, d):
                        copy.start()

                block(s, buf.at[s, d], buf.at[s, 0], dbuf.at[s, d], acc,
                      (dbuf.at[s, 0], cout.at[s, d]), False)

                @pl.when((pos[s] != n - 2) | (d != n - 2))
                def _():
                    give(s, d).start()
        return 0

    lax.fori_loop(1, n - 1, turn, 0)

    for s in range(slots):
        @pl.when(pos[s] == n - 2)
        def _(s=s):
            for copy in back(s):
                copy.wait_recv()
            row_term(s, buf.at[s, n - 1])
            ext_acc[s] = jnp.zeros(ext_acc.shape[1:], jnp.float32)
            block(s, buf.at[s, n - 2], buf.at[s, n - 1], dbuf.at[s, n - 2], ext_acc.at[s],
                  (dbuf.at[s, n - 1], cout.at[s, n - 2]), True)
            give_end(s).start()
            give(s, n - 2).start()

    def collect(d, _):
        for s in range(slots):
            @pl.when(pos[s] + d <= n - 1)
            def _(s=s):
                give(s, d).wait_recv()
                acc[...] += cin[s, d]
        return 0

    lax.fori_loop(1, n - 1, collect, 0)
    for s in range(slots):
        @pl.when(pos[s] == n - 1)
        def _(s=s):
            give_end(s).wait_recv()
            acc[...] += cin[s, n - 1]

    part[0] = acc[0:8, :]
    part[1] = acc[8:16, :]
    here = x * 2 + c

    def swap(k):
        dx, dc = cross[k]
        tx, tc = lax.rem(x + dx, xs), lax.rem(c + dc, 2)
        return remote(part.at[tc], gath.at[here], gs.at[k], gr.at[k], {"views": tx, "rhs": tc})

    for k in range(len(cross)):
        swap(k).start()
    gath[here] = part[c]
    for k in range(len(cross)):
        swap(k).wait()
    direction = dir_ref[...]
    residual = res_ref[...]
    summed = gath[0]
    for k in range(1, 2 * xs):
        summed = summed + gath[k]
    product = summed + ridge_ref[...] * direction

    def total(value):
        return jnp.sum(value, axis=-1, keepdims=True)

    lane = lax.broadcasted_iota(jnp.int32, (8, 128), 1)
    sums = jnp.zeros((8, 128), jnp.float32)
    for k, value in enumerate((residual * residual, direction * product,
                               residual * product, product * product)):
        sums = jnp.where(lane == k, total(value), sums)
    stats[z] = sums

    def spread(k):
        return remote(stats.at[z], stats.at[z], ss.at[k], sr.at[k], {"samples": lax.rem(z + k, n)})

    for k in range(1, n):
        spread(k).start()
    for k in range(1, n):
        spread(k).wait()
    sums = stats[0]
    for k in range(1, n):
        sums = sums + stats[k]
    norm_now, curvature, cross_term, square = (sums[:, k:k + 1] for k in range(4))
    step_size = norm_now / curvature
    norm_next = jnp.maximum(norm_now - step_size * (2.0 * cross_term - step_size * square), 0.0)
    sol_out[...] = sol_ref[...] + step_size * direction
    residual_next = residual - step_size * product
    res_out[...] = residual_next
    dir_out[...] = residual_next + norm_next / norm_now * direction

    for s in range(slots):
        @pl.when(pos[s] < n - 1)
        def _(s=s):
            if slots == 2:
                @pl.when(pos[1 - s] != n - 1)
                def _():
                    forward(s, 0)[0].wait_send()
            else:
                forward(s, 0)[0].wait_send()
            forward(s, 0)[1].wait_send()

        @pl.when(pos[s] == n - 1)
        def _(s=s):
            for copy in back(s):
                copy.wait_send()

        @pl.when(pos[s] == n - 2)
        def _(s=s):
            give_end(s).wait_send()

    def drain(d, _):
        for s in range(slots):
            @pl.when(pos[s] >= d)
            def _(s=s):
                give(s, d).wait_send()

                @pl.when((pos[s] < n - 1) & (d < n - 2))
                def _():
                    for copy in forward(s, d):
                        copy.wait_send()
        return 0

    lax.fori_loop(1, n - 1, drain, 0)


def per_device(
    features, kernel_inverse_scale, view_weight, ridge_term, solution, residual, direction
):
    n = lax.axis_size("samples")
    xs = lax.axis_size("views")
    local_views, rows, feat = features.shape
    cols = direction.shape[1]
    slots = local_views // 2
    tile = math.gcd(rows, 256)
    vmem = pl.BlockSpec(memory_space=pltpu.VMEM)
    smem = pl.BlockSpec(memory_space=pltpu.SMEM)
    dma = pltpu.SemaphoreType.DMA
    f32, bf16 = jnp.float32, jnp.bfloat16
    out = jax.ShapeDtypeStruct((cols, rows), f32)
    outs = pl.pallas_call(
        functools.partial(cg_kernel, n, slots, tile),
        out_shape=(out, out, out),
        in_specs=[smem, smem, pl.BlockSpec(memory_space=pl.ANY), vmem, vmem, vmem, vmem],
        out_specs=(vmem, vmem, vmem),
        scratch_shapes=[
            pltpu.VMEM((slots, n, rows, feat), bf16),
            pltpu.VMEM((slots, n, 2 * cols, rows), bf16),
            pltpu.VMEM((2, cols, rows), f32),
            pltpu.VMEM((2 * cols, rows), f32),
            pltpu.VMEM((slots, 2 * cols, rows), f32),
            pltpu.VMEM((slots, 8, rows), f32),
            pltpu.VMEM((slots, n, 2 * cols, rows), f32),
            pltpu.VMEM((slots, n, 2 * cols, rows), f32),
            pltpu.VMEM((2, cols, rows), f32),
            pltpu.VMEM((2 * xs, cols, rows), f32),
            pltpu.VMEM((n, cols, 128), f32),
            dma((slots,)),
            dma((slots, n)), dma((slots, n)),
            dma((slots, n)), dma((slots, n)),
            dma, dma,
            dma((slots, n)), dma((slots, n)),
            dma((slots,)), dma((slots,)),
            dma((2 * xs - 1,)), dma((2 * xs - 1,)),
            dma((n,)), dma((n,)),
            dma,
        ],
        compiler_params=pltpu.CompilerParams(
            collective_id=0, has_side_effects=True, vmem_limit_bytes=48 * 1024 * 1024
        ),
    )(
        kernel_inverse_scale, view_weight, features, ridge_term[:, None],
        solution.T, residual.T, direction.T,
    )
    return tuple(value.T for value in outs)


def solution(mesh):
    return jax.shard_map(
        per_device,
        mesh=mesh,
        in_specs=(
            P("views", ("groups", "samples"), None),
            P(),
            P(),
            P("rhs"),
            P(("groups", "samples"), "rhs"),
            P(("groups", "samples"), "rhs"),
            P(("groups", "samples"), "rhs"),
        ),
        out_specs=(
            P(("groups", "samples"), "rhs"),
            P(("groups", "samples"), "rhs"),
            P(("groups", "samples"), "rhs"),
        ),
        check_vma=False,
    )
```

time: 144 us -> 51.2 us (0.36)
  waiting for transfers between devices: 74.7 us -> 0 us
  Pallas kernels: 0 us -> 43.5 us
  matrix products: 27.4 us -> 0 us
  blocking collectives: 26.6 us -> 0 us
  other arithmetic: 6.36 us -> 0 us
  starting transfers between devices: 6.01 us -> 0 us
  local copies, waits for them, and re-layouts: 1.53 us -> 6.66 us
    ppermute x6 -> x0, waiting for transfers between devices: 74.7 us -> none  [from_behind(): return lax.ppermute(value, axis, pairs)]
    pallas_call x0 -> x1, Pallas kernels: none -> 43.5 us  [per_device(): pl.pallas_call(functools.partial(cg_kernel, n, slots, tile), out_shape=(o...]
    dot_general x8 -> x0, matrix products: 27.4 us -> none  [the longest x4 24.9 us: tile_product(): jnp.einsum('snt,sgt->sng', features, column_features, preferred_element_t...]
    psum x3 -> x0, blocking collectives: 26.6 us -> none  [the longest x1 10.4 us: per_device(): lax.psum(jnp.sum(residual_next * residual_next, axis=0), 'samples')]
    ppermute x6 -> x0, starting transfers between devices: 6.01 us -> none  [from_behind(): return lax.ppermute(value, axis, pairs)]
    unnamed x15 -> x17, local copies, waits for them, and re-layouts: 0.58 us -> 6.58 us
    reduce_sum x7 -> x0, other arithmetic: 4.83 us -> none  [the longest x3 1.87 us: tile_product(): jnp.sum(jnp.square(column_features.astype(jnp.float32)), axis=-1)]
  transfers between devices with their start and end apart: 6 -> 0, of which waited for: 3 -> 0; matrix products, arithmetic and copies ran while one was open for 0% -> 0% of each run, Pallas kernels for 0% -> 0%
where the time goes in v1:
time: 51.2 us; the launch traced here: 50.8 us
  Pallas kernels  43.5 us (85%)
  local copies, waits for them, and re-layouts  6.66 us (13%)
  between operations  0.66 us (1%)
    pallas_call x1, Pallas kernels, per_device(): pl.pallas_call(functools.partial(cg_kernel, n, slots, tile), out_shape=(o...  43.5 us
    unnamed x17, local copies, waits for them, and re-layouts  6.58 us

profile of v1, /device:TPU:0, one launch (start us, length us, event | category | flops | bytes accessed | tf_op | source)
XLA Modules:
  0.0 50.8 jit_solution(11037578004822537159)
XLA Ops:
  0.6 0.0 copy-start.6
  0.6 0.6 %copy-done.6 = f32[8]{0:T(128)S(1)} copy-done((f32[8]{0:T(128)S(1)}, f32[8]{0:T(128)}, u32[]{:S(2)}) %copy-start.6) | copy-done | bytes 56
  1.3 0.0 copy-start.4
  1.3 0.0 copy-start.5
  1.3 0.1 copy.10.ridge_ref
  1.4 0.6 %copy-done.4 = f32[8]{0:T(128)S(1)} copy-done((f32[8]{0:T(128)S(1)}, f32[8]{0:T(128)}, u32[]{:S(2)}) %copy-start.4) | copy-done | bytes 56
  1.9 0.0 copy-done.5
  2.0 0.0 copy-start
  2.0 1.2 %copy-done = bf16[4,1024,128]{2,1,0:T(8,128)(2,1)S(1)} copy-done((bf16[4,1024,128]{2,1,0:T(8,128)(2,1)S(1)}, bf16[4,1024,128]{2,1,0:T(8,128)(2,1)}, u32[]{:S(2)}) %copy-start) | copy-done | bytes 1048600
  3.2 0.0 copy-start.1
  3.2 0.8 %copy-done.1 = f32[1024,8]{0,1:T(8,128)S(1)} copy-done((f32[1024,8]{0,1:T(8,128)S(1)}, f32[1024,8]{0,1:T(8,128)}, u32[]{:S(2)}) %copy-start.1) | copy-done | bytes 32792
  3.9 0.0 copy-start.2
  3.9 0.8 %copy-done.2 = f32[1024,8]{0,1:T(8,128)S(1)} copy-done((f32[1024,8]{0,1:T(8,128)S(1)}, f32[1024,8]{0,1:T(8,128)}, u32[]{:S(2)}) %copy-start.2) | copy-done | bytes 32792
  4.7 0.0 copy-start.3
  4.7 0.8 %copy-done.3 = f32[1024,8]{0,1:T(8,128)S(1)} copy-done((f32[1024,8]{0,1:T(8,128)S(1)}, f32[1024,8]{0,1:T(8,128)}, u32[]{:S(2)}) %copy-start.3) | copy-done | bytes 32792
  5.5 43.5 %shard_map.94 = (f32[8,1024]{1,0:T(8,128)S(1)}, f32[8,1024]{1,0:T(8,128)S(1)}, f32[8,1024]{1,0:T(8,128)S(1)}) custom-call(f32[8]{0:T(128)S(1)} %copy-done.4, f32[8]{0:T(128)S(1)} %copy-done.5, bf16[4,1024,128]{2,1,0:T(8,128)(2,1)S(1)} %copy-done, f32[8,1]{1,0:T(8,128)S(1)} %copy.10.ridge_ref, f32[8,1024]{1,0:T(8,128)S(1)} %bitcast.10, ...), custom_call_target="tpu_custom_call" | custom-call | tf_op jit(solution)/shard_map/pallas_call | solution.py:299
  49.0 0.6 %copy.14 = f32[1024,8]{0,1:T(8,128)} copy(f32[1024,8]{0,1:T(8,128)S(1)} %bitcast.9) | data formatting | bytes 65536
  49.6 0.6 %copy.15 = f32[1024,8]{0,1:T(8,128)} copy(f32[1024,8]{0,1:T(8,128)S(1)} %bitcast.8) | data formatting | bytes 65536
  50.2 0.6 %copy.16 = f32[1024,8]{0,1:T(8,128)} copy(f32[1024,8]{0,1:T(8,128)S(1)} %bitcast.7) | data formatting | bytes 65536
Async XLA Ops:
  0.6 0.7 %copy-start.6 = (f32[8]{0:T(128)S(1)}, f32[8]{0:T(128)}, u32[]{:S(2)}) copy-start(f32[8]{0:T(128)} %param.10) | copy-start | bytes 100
  1.3 0.7 %copy-start.4 = (f32[8]{0:T(128)S(1)}, f32[8]{0:T(128)}, u32[]{:S(2)}) copy-start(f32[8]{0:T(128)} %scale_ref.1) | copy-start | bytes 100
  1.3 0.7 %copy-start.5 = (f32[8]{0:T(128)S(1)}, f32[8]{0:T(128)}, u32[]{:S(2)}) copy-start(f32[8]{0:T(128)} %weight_ref.1) | copy-start | bytes 100
  2.0 1.2 %copy-start = (bf16[4,1024,128]{2,1,0:T(8,128)(2,1)S(1)}, bf16[4,1024,128]{2,1,0:T(8,128)(2,1)}, u32[]{:S(2)}) copy-start(bf16[4,1024,128]{2,1,0:T(8,128)(2,1)} %feats_ref.1) | copy-start | bytes 3145732
  3.2 0.8 %copy-start.1 = (f32[1024,8]{0,1:T(8,128)S(1)}, f32[1024,8]{0,1:T(8,128)}, u32[]{:S(2)}) copy-start(f32[1024,8]{0,1:T(8,128)} %param.11) | copy-start | bytes 98308
  3.9 0.8 %copy-start.2 = (f32[1024,8]{0,1:T(8,128)S(1)}, f32[1024,8]{0,1:T(8,128)}, u32[]{:S(2)}) copy-start(f32[1024,8]{0,1:T(8,128)} %param.12) | copy-start | bytes 98308
  4.7 0.8 %copy-start.3 = (f32[1024,8]{0,1:T(8,128)S(1)}, f32[1024,8]{0,1:T(8,128)}, u32[]{:S(2)}) copy-start(f32[1024,8]{0,1:T(8,128)} %param.13) | copy-start | bytes 98308

commit v2 on v1

--- a/solution.py
+++ b/solution.py
@@ -14,10 +14,11 @@
 
 def cg_kernel(
     n, slots, tile,
-    scale_ref, weight_ref, feats_ref, ridge_ref, sol_ref, res_ref, dir_ref,
-    sol_out, res_out, dir_out,
+    scale_hbm, weight_hbm, ridge_hbm, feats_ref, res_hbm, dir_hbm,
+    product_out, step_out, ratio_out,
+    scale_ref, weight_ref, ridge_ref, res_ref,
     buf, dbuf, dpair, acc, ext_acc, norms, cout, cin, part, gath, stats,
-    load_sem, fs, fr, ds, dr, ps, pr, cs, cr, es, er, gs, gr, ss, sr, dir_stage,
+    load_sem, small_sem, fs, fr, ds, dr, ps, pr, cs, cr, es, gs, gr, ss, sr,
 ):
     z = lax.axis_index("samples")
     x = lax.axis_index("views")
@@ -27,6 +28,7 @@
     first_view = x * local_views
     rows = feats_ref.shape[1]
     half = local_views // 2
+    pieces = [pl.ds(k * tile, tile) for k in range(rows // tile)]
 
     if slots == 2:
         view = [c, half + c]
@@ -40,8 +42,17 @@
     def load(s):
         return pltpu.make_async_copy(feats_ref.at[view[s]], buf.at[s, 0], load_sem.at[s])
 
+    fetch = [
+        pltpu.make_async_copy(src, dst, small_sem.at[k])
+        for k, (src, dst) in enumerate((
+            (dir_hbm, dpair.at[c]), (scale_hbm, scale_ref), (weight_hbm, weight_ref),
+            (ridge_hbm, ridge_ref), (res_hbm, res_ref),
+        ))
+    ]
     for s in range(slots):
         load(s).start()
+    for copy in fetch:
+        copy.start()
 
     barrier = pltpu.get_barrier_semaphore()
     peers = [{"samples": lax.rem(z + k, n)} for k in range(1, n)]
@@ -61,14 +72,20 @@
         return {"samples": lax.rem(z + sgn[s] * steps + 2 * n, n)}
 
     def forward(s, d):
-        return (
-            remote(buf.at[s, d], buf.at[s, d + 1], fs.at[s, d], fr.at[s, d + 1], ahead(s, 1)),
+        return tuple(
+            remote(buf.at[s, d, at], buf.at[s, d + 1, at],
+                   fs.at[s, d, k], fr.at[s, d + 1, k], ahead(s, 1))
+            for k, at in enumerate(pieces)
+        ) + (
             remote(dbuf.at[s, d], dbuf.at[s, d + 1], ds.at[s, d], dr.at[s, d + 1], ahead(s, 1)),
         )
 
     def back(s):
-        return (
-            remote(buf.at[s, 0], buf.at[s, n - 1], fs.at[s, n - 1], fr.at[s, n - 1], ahead(s, -1)),
+        return tuple(
+            remote(buf.at[s, 0, at], buf.at[s, n - 1, at],
+                   fs.at[s, n - 1, k], fr.at[s, n - 1, k], ahead(s, -1))
+            for k, at in enumerate(pieces)
+        ) + (
             remote(dbuf.at[s, 0], dbuf.at[s, n - 1], ds.at[s, n - 1], dr.at[s, n - 1], ahead(s, -1)),
         )
 
@@ -78,18 +95,18 @@
     def give_end(s):
         return remote(ext_acc.at[s], cin.at[s, n - 1], es.at[s], cr.at[s, n - 1], ahead(s, 1))
 
-    pair = remote(dir_ref, dpair.at[c], ps, pr, {"rhs": 1 - c})
+    for copy in fetch:
+        copy.wait()
+    pair = remote(dpair.at[c], dpair.at[c], ps, pr, {"rhs": 1 - c})
     pair.start()
-    stage = pltpu.make_async_copy(dir_ref, dpair.at[c], dir_stage)
-    stage.start()
     for s in range(slots):
         load(s).wait()
 
         @pl.when(pos[s] < n - 1)
         def _(s=s):
-            forward(s, 0)[0].start()
-
-    stage.wait()
+            for copy in forward(s, 0)[:-1]:
+                copy.start()
+
     pair.wait()
     low = jnp.concatenate([dpair[0], dpair[1]], axis=0).astype(jnp.bfloat16)
     for s in range(slots):
@@ -97,7 +114,7 @@
 
         @pl.when(pos[s] < n - 1)
         def _(s=s):
-            forward(s, 0)[1].start()
+            forward(s, 0)[-1].start()
 
     def consts(s):
         index = first_view + view[s]
@@ -113,25 +130,26 @@
         )
         norms[s] = low_weight - rate * sums
 
-    def block(s, jb, ib, jd, i_sum, j_sum, add_j):
+    def block(s, jb, ib, jd, at, i_sum, j_sum, add_j):
         rate, _ = consts(s)
-
+        fj = jb[at, :]
+        inner = lax.dot_general(fj, ib[...], LANES, preferred_element_type=jnp.float32)
+        wide = fj.astype(jnp.float32)
+        column = -rate * jnp.sum(wide * wide, axis=-1, keepdims=True)
+        power = (2.0 * rate) * inner + norms[s, 0:1, :] + column
+        kern = jnp.exp2(power).astype(jnp.bfloat16)
+        i_sum[...] += jnp.dot(jd[:, at], kern, preferred_element_type=jnp.float32)
+        if j_sum is not None:
+            (idir, target) = j_sum
+            term = lax.dot_general(idir[...], kern, LANES, preferred_element_type=jnp.float32)
+            if add_j:
+                target[:, at] += term
+            else:
+                target[:, at] = term
+
+    def each_piece(run):
         def step(t, _):
-            at = pl.ds(pl.multiple_of(t * tile, tile), tile)
-            fj = jb[at, :]
-            inner = lax.dot_general(fj, ib[...], LANES, preferred_element_type=jnp.float32)
-            wide = fj.astype(jnp.float32)
-            column = -rate * jnp.sum(wide * wide, axis=-1, keepdims=True)
-            power = (2.0 * rate) * inner + norms[s, 0:1, :] + column
-            kern = jnp.exp2(power).astype(jnp.bfloat16)
-            i_sum[...] += jnp.dot(jd[:, at], kern, preferred_element_type=jnp.float32)
-            if j_sum is not None:
-                (idir, target) = j_sum
-                term = lax.dot_general(idir[...], kern, LANES, preferred_element_type=jnp.float32)
-                if add_j:
-                    target[:, at] += term
-                else:
-                    target[:, at] = term
+            run(pl.ds(pl.multiple_of(t * tile, tile), tile))
             return 0
 
         lax.fori_loop(0, rows // tile, step, 0)
@@ -139,34 +157,44 @@
     acc[...] = jnp.zeros_like(acc)
     for s in range(slots):
         row_term(s, buf.at[s, 0])
-        block(s, buf.at[s, 0], buf.at[s, 0], dbuf.at[s, 0], acc, None, False)
+        each_piece(functools.partial(
+            lambda s, at: block(s, buf.at[s, 0], buf.at[s, 0], dbuf.at[s, 0], at, acc, None, False),
+            s))
 
     for s in range(slots):
         @pl.when(pos[s] == n - 1)
         def _(s=s):
             if slots == 2:
-                forward(1 - s, 0)[0].wait_send()
+                for copy in forward(1 - s, 0)[:-1]:
+                    copy.wait_send()
             for copy in back(s):
                 copy.start()
 
     def turn(d, _):
-        for s in range(slots):
-            @pl.when(pos[s] >= d)
-            def _(s=s):
-                for copy in forward(s, d - 1):
-                    copy.wait_recv()
-
-                @pl.when((pos[s] < n - 1) & (d < n - 2))
-                def _():
-                    for copy in forward(s, d):
-                        copy.start()
-
-                block(s, buf.at[s, d], buf.at[s, 0], dbuf.at[s, d], acc,
-                      (dbuf.at[s, 0], cout.at[s, d]), False)
-
-                @pl.when((pos[s] != n - 2) | (d != n - 2))
-                def _():
-                    give(s, d).start()
+        for k, at in enumerate(pieces):
+            for s in range(slots):
+                @pl.when(pos[s] >= d)
+                def _(s=s, k=k, at=at):
+                    forward(s, d - 1)[k].wait_recv()
+
+                    @pl.when((pos[s] < n - 1) & (d < n - 2))
+                    def _():
+                        forward(s, d)[k].start()
+
+                    if k == 0:
+                        forward(s, d - 1)[-1].wait_recv()
+
+                        @pl.when((pos[s] < n - 1) & (d < n - 2))
+                        def _():
+                            forward(s, d)[-1].start()
+
+                    block(s, buf.at[s, d], buf.at[s, 0], dbuf.at[s, d], at, acc,
+                          (dbuf.at[s, 0], cout.at[s, d]), False)
+
+                    if k == len(pieces) - 1:
+                        @pl.when((pos[s] != n - 2) | (d != n - 2))
+                        def _():
+                            give(s, d).start()
         return 0
 
     lax.fori_loop(1, n - 1, turn, 0)
@@ -178,8 +206,9 @@
                 copy.wait_recv()
             row_term(s, buf.at[s, n - 1])
             ext_acc[s] = jnp.zeros(ext_acc.shape[1:], jnp.float32)
-            block(s, buf.at[s, n - 2], buf.at[s, n - 1], dbuf.at[s, n - 2], ext_acc.at[s],
-                  (dbuf.at[s, n - 1], cout.at[s, n - 2]), True)
+            each_piece(lambda at: block(
+                s, buf.at[s, n - 2], buf.at[s, n - 1], dbuf.at[s, n - 2], at, ext_acc.at[s],
+                (dbuf.at[s, n - 1], cout.at[s, n - 2]), True))
             give_end(s).start()
             give(s, n - 2).start()
 
@@ -212,12 +241,17 @@
     gath[here] = part[c]
     for k in range(len(cross)):
         swap(k).wait()
-    direction = dir_ref[...]
+    direction = dpair[c]
     residual = res_ref[...]
     summed = gath[0]
     for k in range(1, 2 * xs):
         summed = summed + gath[k]
-    product = summed + ridge_ref[...] * direction
+    row = lax.broadcasted_iota(jnp.int32, (8, 1), 0)
+    ridge = jnp.zeros((8, 1), jnp.float32)
+    for k in range(8):
+        ridge = jnp.where(row == k, ridge_ref[k], ridge)
+    product = summed + ridge * direction
+    product_out[...] = product
 
     def total(value):
         return jnp.sum(value, axis=-1, keepdims=True)
@@ -242,10 +276,8 @@
     norm_now, curvature, cross_term, square = (sums[:, k:k + 1] for k in range(4))
     step_size = norm_now / curvature
     norm_next = jnp.maximum(norm_now - step_size * (2.0 * cross_term - step_size * square), 0.0)
-    sol_out[...] = sol_ref[...] + step_size * direction
-    residual_next = residual - step_size * product
-    res_out[...] = residual_next
-    dir_out[...] = residual_next + norm_next / norm_now * direction
+    step_out[...] = jnp.broadcast_to(step_size, step_out.shape)
+    ratio_out[...] = jnp.broadcast_to(norm_next / norm_now, ratio_out.shape)
 
     for s in range(slots):
         @pl.when(pos[s] < n - 1)
@@ -253,10 +285,12 @@
             if slots == 2:
                 @pl.when(pos[1 - s] != n - 1)
                 def _():
-                    forward(s, 0)[0].wait_send()
+                    for copy in forward(s, 0)[:-1]:
+                        copy.wait_send()
             else:
-                forward(s, 0)[0].wait_send()
-            forward(s, 0)[1].wait_send()
+                for copy in forward(s, 0)[:-1]:
+                    copy.wait_send()
+            forward(s, 0)[-1].wait_send()
 
         @pl.when(pos[s] == n - 1)
         def _(s=s):
@@ -290,18 +324,23 @@
     local_views, rows, feat = features.shape
     cols = direction.shape[1]
     slots = local_views // 2
-    tile = math.gcd(rows, 256)
+    tile = math.gcd(rows, 512)
+    chunks = rows // tile
     vmem = pl.BlockSpec(memory_space=pltpu.VMEM)
-    smem = pl.BlockSpec(memory_space=pltpu.SMEM)
+    hbm = pl.BlockSpec(memory_space=pltpu.HBM)
     dma = pltpu.SemaphoreType.DMA
     f32, bf16 = jnp.float32, jnp.bfloat16
     out = jax.ShapeDtypeStruct((cols, rows), f32)
-    outs = pl.pallas_call(
+    product, step_size, ratio = pl.pallas_call(
         functools.partial(cg_kernel, n, slots, tile),
         out_shape=(out, out, out),
-        in_specs=[smem, smem, pl.BlockSpec(memory_space=pl.ANY), vmem, vmem, vmem, vmem],
+        in_specs=[hbm] * 6,
         out_specs=(vmem, vmem, vmem),
         scratch_shapes=[
+            pltpu.SMEM(kernel_inverse_scale.shape, f32),
+            pltpu.SMEM(view_weight.shape, f32),
+            pltpu.SMEM(ridge_term.shape, f32),
+            pltpu.VMEM((cols, rows), f32),
             pltpu.VMEM((slots, n, rows, feat), bf16),
             pltpu.VMEM((slots, n, 2 * cols, rows), bf16),
             pltpu.VMEM((2, cols, rows), f32),
@@ -314,23 +353,26 @@
             pltpu.VMEM((2 * xs, cols, rows), f32),
             pltpu.VMEM((n, cols, 128), f32),
             dma((slots,)),
-            dma((slots, n)), dma((slots, n)),
+            dma((5,)),
+            dma((slots, n, chunks)), dma((slots, n, chunks)),
             dma((slots, n)), dma((slots, n)),
             dma, dma,
             dma((slots, n)), dma((slots, n)),
-            dma((slots,)), dma((slots,)),
+            dma((slots,)),
             dma((2 * xs - 1,)), dma((2 * xs - 1,)),
             dma((n,)), dma((n,)),
-            dma,
         ],
         compiler_params=pltpu.CompilerParams(
-            collective_id=0, has_side_effects=True, vmem_limit_bytes=48 * 1024 * 1024
+            collective_id=0, has_side_effects=True, vmem_limit_bytes=63 * 1024 * 1024
         ),
     )(
-        kernel_inverse_scale, view_weight, features, ridge_term[:, None],
-        solution.T, residual.T, direction.T,
+        kernel_inverse_scale, view_weight, ridge_term, features, residual.T, direction.T,
     )
-    return tuple(value.T for value in outs)
+    product, step_size, ratio = product.T, step_size.T, ratio.T
+    solution_next = solution + step_size * direction
+    residual_next = residual - step_size * product
+    direction_next = residual_next + ratio * direction
+    return (solution_next, residual_next, direction_next)
 
 
 def solution(mesh):

time: 51.2 us -> 40.7 us (0.79)
  local copies, waits for them, and re-layouts: 6.66 us -> 0.01 us
  Pallas kernels: 43.5 us -> 38.4 us
  other arithmetic: 0 us -> 1.44 us
    unnamed x17 -> x6, local copies, waits for them, and re-layouts: 6.58 us -> 0.01 us
    pallas_call x1, Pallas kernels: 43.5 us -> 38.4 us  [per_device(): pl.pallas_call(functools.partial(cg_kernel, n, slots, tile), out_shape=(o...]
    add x0 -> x1, other arithmetic: none -> 1.44 us  [per_device(): direction_next = residual_next + ratio * direction]
where the time goes in v2:
time: 40.7 us; the launch traced here: 40.5 us
  Pallas kernels  38.4 us (94%)
  other arithmetic  1.44 us (4%)
  between operations  0.69 us (2%)
    pallas_call x1, Pallas kernels, per_device(): pl.pallas_call(functools.partial(cg_kernel, n, slots, tile), out_shape=(o...  38.4 us
    add x1, other arithmetic, per_device(): direction_next = residual_next + ratio * direction  1.44 us

profile of v2, /device:TPU:0, one launch (start us, length us, event | category | flops | bytes accessed | tf_op | source)
XLA Modules:
  0.0 40.5 jit_solution(4068141136403564202)
XLA Ops:
  0.6 0.0 copy-start
  0.6 0.0 copy-start.1
  0.7 0.0 copy-start.2
  0.7 38.4 %shard_map.94 = (f32[8,1024]{1,0:T(8,128)}, f32[8,1024]{1,0:T(8,128)}, f32[8,1024]{1,0:T(8,128)}) custom-call(f32[8]{0:T(128)} %scale_hbm.1, f32[8]{0:T(128)} %weight_hbm.1, f32[8]{0:T(128)} %ridge_hbm.1, bf16[4,1024,128]{2,1,0:T(8,128)(2,1)} %feats_ref.1, f32[8,1024]{1,0:T(8,128)} %bitcast.18, f32[8,1024]{1,0:T(8,128)} %bitcast.17), custom_call_target="tpu_custom_call" | custom-call | tf_op jit(solution)/shard_map/pallas_call | solution.py:334
  39.0 0.0 copy-done
  39.0 0.0 copy-done.1
  39.1 0.0 copy-done.2
  39.1 1.4 %fusion = (f32[1024,8]{0,1:T(8,128)}, f32[1024,8]{0,1:T(8,128)}, f32[1024,8]{0,1:T(8,128)}) fusion(f32[1024,8]{0,1:T(8,128)S(1)} %copy-done, f32[8,1024]{1,0:T(8,128)} %get-tuple-element.8, f32[1024,8]{0,1:T(8,128)S(1)} %copy-done.1, f32[8,1024]{1,0:T(8,128)} %get-tuple-element.7, f32[8,1024]{1,0:T(8,128)} %get-tuple-element.6, f32[1024,8]{0,1:T(8,128)S(1)} %copy-done.2), kind=kLoop, calls=%fused_computation.1 | loop fusion | flops 49152 | bytes 294912 | tf_op jit(solution)/shard_map/add | solution.py:374
Async XLA Ops:
  0.6 38.4 %copy-start = (f32[1024,8]{0,1:T(8,128)S(1)}, f32[1024,8]{0,1:T(8,128)}, u32[]{:S(2)}) copy-start(f32[1024,8]{0,1:T(8,128)} %param.13) | copy-start | bytes 98308
  0.6 38.4 %copy-start.1 = (f32[1024,8]{0,1:T(8,128)S(1)}, f32[1024,8]{0,1:T(8,128)}, u32[]{:S(2)}) copy-start(f32[1024,8]{0,1:T(8,128)} %param.12) | copy-start | bytes 98308
  0.7 38.4 %copy-start.2 = (f32[1024,8]{0,1:T(8,128)S(1)}, f32[1024,8]{0,1:T(8,128)}, u32[]{:S(2)}) copy-start(f32[1024,8]{0,1:T(8,128)} %param.11) | copy-start | bytes 98308

commit v3 on v2

--- a/solution.py
+++ b/solution.py
@@ -17,7 +17,7 @@
     scale_hbm, weight_hbm, ridge_hbm, feats_ref, res_hbm, dir_hbm,
     product_out, step_out, ratio_out,
     scale_ref, weight_ref, ridge_ref, res_ref,
-    buf, dbuf, dpair, acc, ext_acc, norms, cout, cin, part, gath, stats,
+    buf, dbuf, dpair, acc, ext_acc, norms, cout, cin, part, gath, tot, stats,
     load_sem, small_sem, fs, fr, ds, dr, ps, pr, cs, cr, es, gs, gr, ss, sr,
 ):
     z = lax.axis_index("samples")
@@ -55,12 +55,18 @@
         copy.start()
 
     barrier = pltpu.get_barrier_semaphore()
-    peers = [{"samples": lax.rem(z + k, n)} for k in range(1, n)]
+    sides = (z > 0).astype(jnp.int32) + (z < n - 1).astype(jnp.int32)
     cross = [(dx, dc) for dx in range(xs) for dc in range(2) if (dx, dc) != (0, 0)]
-    peers += [{"views": lax.rem(x + dx, xs), "rhs": lax.rem(c + dc, 2)} for dx, dc in cross]
-    for peer in peers:
-        pl.semaphore_signal(barrier, inc=1, device_id=peer, device_id_type=MESH)
-    pl.semaphore_wait(barrier, len(peers))
+    for near, there in ((z - 1, z > 0), (z + 1, z < n - 1)):
+        @pl.when(there)
+        def _(near=near):
+            pl.semaphore_signal(
+                barrier, inc=1, device_id={"samples": near}, device_id_type=MESH)
+    for dx, dc in cross:
+        pl.semaphore_signal(
+            barrier, inc=1, device_id_type=MESH,
+            device_id={"views": lax.rem(x + dx, xs), "rhs": lax.rem(c + dc, 2)})
+    pl.semaphore_wait(barrier, len(cross) + sides)
 
     def remote(src, dst, send, recv, target):
         return pltpu.make_async_remote_copy(
@@ -89,11 +95,30 @@
             remote(dbuf.at[s, 0], dbuf.at[s, n - 1], ds.at[s, n - 1], dr.at[s, n - 1], ahead(s, -1)),
         )
 
-    def give(s, d):
-        return remote(cout.at[s, d], cin.at[s, d], cs.at[s, d], cr.at[s, d], ahead(s, -d))
+    here = x * 2 + c
+    owners = [(dx, oc) for dx in range(xs) for oc in range(2)]
+
+    def give(s, d, k):
+        return [
+            remote(cout.at[s, d, pl.ds(8 * oc, 8), pieces[k]], cin.at[s, d, here, :, pieces[k]],
+                   cs.at[s, d, k, j], cr.at[s, d, k, here],
+                   {"views": lax.rem(x + dx, xs), "rhs": oc} | ahead(s, -d))
+            for j, (dx, oc) in enumerate(owners)
+        ]
 
     def give_end(s):
-        return remote(ext_acc.at[s], cin.at[s, n - 1], es.at[s], cr.at[s, n - 1], ahead(s, 1))
+        return [
+            remote(ext_acc.at[s, pl.ds(8 * oc, 8)], cin.at[s, n - 1, here],
+                   es.at[s, j], cr.at[s, n - 1, 0, here],
+                   {"views": lax.rem(x + dx, xs), "rhs": oc} | ahead(s, 1))
+            for j, (dx, oc) in enumerate(owners)
+        ]
+
+    def taken(s, d, k, source):
+        at = pieces[k] if d is not None else pl.ds(0, rows)
+        d = n - 1 if d is None else d
+        return remote(cout.at[s, d, pl.ds(0, 8), at], cin.at[s, d, source, :, at],
+                      cs.at[s, d, k, 0], cr.at[s, d, k, source], ahead(s, 1))
 
     for copy in fetch:
         copy.wait()
@@ -164,11 +189,12 @@
     for s in range(slots):
         @pl.when(pos[s] == n - 1)
         def _(s=s):
-            if slots == 2:
-                for copy in forward(1 - s, 0)[:-1]:
-                    copy.wait_send()
-            for copy in back(s):
-                copy.start()
+            moves = back(s)
+            moves[-1].start()
+            for k in range(len(pieces)):
+                if slots == 2:
+                    forward(1 - s, 0)[k].wait_send()
+                moves[k].start()
 
     def turn(d, _):
         for k, at in enumerate(pieces):
@@ -191,10 +217,10 @@
                     block(s, buf.at[s, d], buf.at[s, 0], dbuf.at[s, d], at, acc,
                           (dbuf.at[s, 0], cout.at[s, d]), False)
 
-                    if k == len(pieces) - 1:
-                        @pl.when((pos[s] != n - 2) | (d != n - 2))
-                        def _():
-                            give(s, d).start()
+                    @pl.when((pos[s] != n - 2) | (d != n - 2))
+                    def _():
+                        for copy in give(s, d, k):
+                            copy.start()
         return 0
 
     lax.fori_loop(1, n - 1, turn, 0)
@@ -206,30 +232,16 @@
                 copy.wait_recv()
             row_term(s, buf.at[s, n - 1])
             ext_acc[s] = jnp.zeros(ext_acc.shape[1:], jnp.float32)
-            each_piece(lambda at: block(
-                s, buf.at[s, n - 2], buf.at[s, n - 1], dbuf.at[s, n - 2], at, ext_acc.at[s],
-                (dbuf.at[s, n - 1], cout.at[s, n - 2]), True))
-            give_end(s).start()
-            give(s, n - 2).start()
-
-    def collect(d, _):
-        for s in range(slots):
-            @pl.when(pos[s] + d <= n - 1)
-            def _(s=s):
-                give(s, d).wait_recv()
-                acc[...] += cin[s, d]
-        return 0
-
-    lax.fori_loop(1, n - 1, collect, 0)
-    for s in range(slots):
-        @pl.when(pos[s] == n - 1)
-        def _(s=s):
-            give_end(s).wait_recv()
-            acc[...] += cin[s, n - 1]
+            for k, at in enumerate(pieces):
+                block(s, buf.at[s, n - 2], buf.at[s, n - 1], dbuf.at[s, n - 2], at, ext_acc.at[s],
+                      (dbuf.at[s, n - 1], cout.at[s, n - 2]), True)
+                for copy in give(s, n - 2, k):
+                    copy.start()
+            for copy in give_end(s):
+                copy.start()
 
     part[0] = acc[0:8, :]
     part[1] = acc[8:16, :]
-    here = x * 2 + c
 
     def swap(k):
         dx, dc = cross[k]
@@ -239,6 +251,10 @@
     for k in range(len(cross)):
         swap(k).start()
     gath[here] = part[c]
+
+    def place(s, core):
+        return pos[s] if slots == 2 else z * (1 - core) + (n - 1 - z) * core
+
     for k in range(len(cross)):
         swap(k).wait()
     direction = dpair[c]
@@ -246,6 +262,30 @@
     summed = gath[0]
     for k in range(1, 2 * xs):
         summed = summed + gath[k]
+    tot[...] = summed
+
+    def collect(d, _):
+        for s in range(slots):
+            for core in range(2):
+                @pl.when(place(s, core) + d <= n - 1)
+                def _(s=s, core=core):
+                    for other in range(xs):
+                        source = other * 2 + core
+                        for k in range(len(pieces)):
+                            taken(s, d, k, source).wait_recv()
+                        tot[...] += cin[s, d, source]
+        return 0
+
+    lax.fori_loop(1, n - 1, collect, 0)
+    for s in range(slots):
+        for core in range(2):
+            @pl.when(place(s, core) == n - 1)
+            def _(s=s, core=core):
+                for other in range(xs):
+                    source = other * 2 + core
+                    taken(s, None, 0, source).wait_recv()
+                    tot[...] += cin[s, n - 1, source]
+    summed = tot[...]
     row = lax.broadcasted_iota(jnp.int32, (8, 1), 0)
     ridge = jnp.zeros((8, 1), jnp.float32)
     for k in range(8):
@@ -299,13 +339,16 @@
 
         @pl.when(pos[s] == n - 2)
         def _(s=s):
-            give_end(s).wait_send()
+            for copy in give_end(s):
+                copy.wait_send()
 
     def drain(d, _):
         for s in range(slots):
             @pl.when(pos[s] >= d)
             def _(s=s):
-                give(s, d).wait_send()
+                for k in range(len(pieces)):
+                    for copy in give(s, d, k):
+                        copy.wait_send()
 
                 @pl.when((pos[s] < n - 1) & (d < n - 2))
                 def _():
@@ -348,17 +391,18 @@
             pltpu.VMEM((slots, 2 * cols, rows), f32),
             pltpu.VMEM((slots, 8, rows), f32),
             pltpu.VMEM((slots, n, 2 * cols, rows), f32),
-            pltpu.VMEM((slots, n, 2 * cols, rows), f32),
+            pltpu.VMEM((slots, n, 2 * xs, cols, rows), f32),
             pltpu.VMEM((2, cols, rows), f32),
             pltpu.VMEM((2 * xs, cols, rows), f32),
+            pltpu.VMEM((cols, rows), f32),
             pltpu.VMEM((n, cols, 128), f32),
             dma((slots,)),
             dma((5,)),
             dma((slots, n, chunks)), dma((slots, n, chunks)),
             dma((slots, n)), dma((slots, n)),
             dma, dma,
-            dma((slots, n)), dma((slots, n)),
-            dma((slots,)),
+            dma((slots, n, chunks, 2 * xs)), dma((slots, n, chunks, 2 * xs)),
+            dma((slots, 2 * xs)),
             dma((2 * xs - 1,)), dma((2 * xs - 1,)),
             dma((n,)), dma((n,)),
         ],

time: 40.7 us -> 42.2 us (1.037)
  Pallas kernels: 38.4 us -> 39.9 us
    pallas_call x1, Pallas kernels: 38.4 us -> 39.9 us  [per_device(): pl.pallas_call(functools.partial(cg_kernel, n, slots, tile), out_shape=(o...]
where the time goes in v3:
time: 42.2 us; the launch traced here: 42 us
  Pallas kernels  39.9 us (95%)
  other arithmetic  1.44 us (3%)
  between operations  0.69 us (2%)
    pallas_call x1, Pallas kernels, per_device(): pl.pallas_call(functools.partial(cg_kernel, n, slots, tile), out_shape=(o...  39.9 us
    add x1, other arithmetic, per_device(): direction_next = residual_next + ratio * direction  1.44 us

profile of v3, /device:TPU:0, one launch (start us, length us, event | category | flops | bytes accessed | tf_op | source)
XLA Modules:
  0.0 42.0 jit_solution(5714427251614196788)
XLA Ops:
  0.6 0.0 copy-start
  0.6 0.0 copy-start.1
  0.7 0.0 copy-start.2
  0.7 39.9 %shard_map.94 = (f32[8,1024]{1,0:T(8,128)}, f32[8,1024]{1,0:T(8,128)}, f32[8,1024]{1,0:T(8,128)}) custom-call(f32[8]{0:T(128)} %scale_hbm.1, f32[8]{0:T(128)} %weight_hbm.1, f32[8]{0:T(128)} %ridge_hbm.1, bf16[4,1024,128]{2,1,0:T(8,128)(2,1)} %feats_ref.1, f32[8,1024]{1,0:T(8,128)} %bitcast.18, f32[8,1024]{1,0:T(8,128)} %bitcast.17), custom_call_target="tpu_custom_call" | custom-call | tf_op jit(solution)/shard_map/pallas_call | solution.py:377
  40.5 0.0 copy-done
  40.6 0.0 copy-done.1
  40.6 0.0 copy-done.2
  40.6 1.4 %fusion = (f32[1024,8]{0,1:T(8,128)}, f32[1024,8]{0,1:T(8,128)}, f32[1024,8]{0,1:T(8,128)}) fusion(f32[1024,8]{0,1:T(8,128)S(1)} %copy-done, f32[8,1024]{1,0:T(8,128)} %get-tuple-element.8, f32[1024,8]{0,1:T(8,128)S(1)} %copy-done.1, f32[8,1024]{1,0:T(8,128)} %get-tuple-element.7, f32[8,1024]{1,0:T(8,128)} %get-tuple-element.6, f32[1024,8]{0,1:T(8,128)S(1)} %copy-done.2), kind=kLoop, calls=%fused_computation.1 | loop fusion | flops 49152 | bytes 294912 | tf_op jit(solution)/shard_map/add | solution.py:418
Async XLA Ops:
  0.6 39.9 %copy-start = (f32[1024,8]{0,1:T(8,128)S(1)}, f32[1024,8]{0,1:T(8,128)}, u32[]{:S(2)}) copy-start(f32[1024,8]{0,1:T(8,128)} %param.13) | copy-start | bytes 98308
  0.6 39.9 %copy-start.1 = (f32[1024,8]{0,1:T(8,128)S(1)}, f32[1024,8]{0,1:T(8,128)}, u32[]{:S(2)}) copy-start(f32[1024,8]{0,1:T(8,128)} %param.12) | copy-start | bytes 98308
  0.7 39.9 %copy-start.2 = (f32[1024,8]{0,1:T(8,128)S(1)}, f32[1024,8]{0,1:T(8,128)}, u32[]{:S(2)}) copy-start(f32[1024,8]{0,1:T(8,128)} %param.11) | copy-start | bytes 98308

commit v4 on v3

--- a/solution.py
+++ b/solution.py
@@ -17,8 +17,8 @@
     scale_hbm, weight_hbm, ridge_hbm, feats_ref, res_hbm, dir_hbm,
     product_out, step_out, ratio_out,
     scale_ref, weight_ref, ridge_ref, res_ref,
-    buf, dbuf, dpair, acc, ext_acc, norms, cout, cin, part, gath, tot, stats,
-    load_sem, small_sem, fs, fr, ds, dr, ps, pr, cs, cr, es, gs, gr, ss, sr,
+    buf, dbuf, dpair, acc, ext_acc, norms, norms_end, cout, cin, late, part, gath, tot, stats,
+    load_sem, small_sem, fs, fr, ds, dr, ps, pr, cs, cr, ls, lr, gs, gr, ss, sr,
 ):
     z = lax.axis_index("samples")
     x = lax.axis_index("views")
@@ -99,26 +99,30 @@
     owners = [(dx, oc) for dx in range(xs) for oc in range(2)]
 
     def give(s, d, k):
+        return remote(cout.at[s, d, :, pieces[k]], cin.at[s, d, :, pieces[k]],
+                      cs.at[s, d, k], cr.at[s, d, k], ahead(s, -d))
+
+    def give_last(s, k):
         return [
-            remote(cout.at[s, d, pl.ds(8 * oc, 8), pieces[k]], cin.at[s, d, here, :, pieces[k]],
-                   cs.at[s, d, k, j], cr.at[s, d, k, here],
-                   {"views": lax.rem(x + dx, xs), "rhs": oc} | ahead(s, -d))
+            remote(cout.at[s, n - 2, pl.ds(8 * oc, 8), pieces[k]],
+                   late.at[s, 0, here, :, pieces[k]],
+                   ls.at[s, 0, k, j], lr.at[s, 0, k, here],
+                   {"views": lax.rem(x + dx, xs), "rhs": oc} | ahead(s, 2 - n))
             for j, (dx, oc) in enumerate(owners)
         ]
 
     def give_end(s):
         return [
-            remote(ext_acc.at[s, pl.ds(8 * oc, 8)], cin.at[s, n - 1, here],
-                   es.at[s, j], cr.at[s, n - 1, 0, here],
+            remote(ext_acc.at[s, pl.ds(8 * oc, 8)], late.at[s, 1, here],
+                   ls.at[s, 1, 0, j], lr.at[s, 1, 0, here],
                    {"views": lax.rem(x + dx, xs), "rhs": oc} | ahead(s, 1))
             for j, (dx, oc) in enumerate(owners)
         ]
 
-    def taken(s, d, k, source):
-        at = pieces[k] if d is not None else pl.ds(0, rows)
-        d = n - 1 if d is None else d
-        return remote(cout.at[s, d, pl.ds(0, 8), at], cin.at[s, d, source, :, at],
-                      cs.at[s, d, k, 0], cr.at[s, d, k, source], ahead(s, 1))
+    def taken(s, e, k, source):
+        at = pl.ds(0, rows) if e else pieces[k]
+        return remote(cout.at[s, n - 2, pl.ds(0, 8), at], late.at[s, e, source, :, at],
+                      ls.at[s, e, k, 0], lr.at[s, e, k, source], ahead(s, 1))
 
     for copy in fetch:
         copy.wait()
@@ -146,7 +150,7 @@
         rate = scale_ref[index] * math.log2(math.e)
         return rate, jnp.log2(jnp.full((1, 1), weight_ref[index], jnp.float32))
 
-    def row_term(s, slot_ref):
+    def row_term(s, slot_ref, norms):
         rate, low_weight = consts(s)
         feats = slot_ref[...].astype(jnp.float32)
         sums = lax.dot_general(
@@ -155,7 +159,7 @@
         )
         norms[s] = low_weight - rate * sums
 
-    def block(s, jb, ib, jd, at, i_sum, j_sum, add_j):
+    def block(s, jb, ib, jd, at, i_sum, j_sum, add_j, norms):
         rate, _ = consts(s)
         fj = jb[at, :]
         inner = lax.dot_general(fj, ib[...], LANES, preferred_element_type=jnp.float32)
@@ -181,9 +185,10 @@
 
     acc[...] = jnp.zeros_like(acc)
     for s in range(slots):
-        row_term(s, buf.at[s, 0])
+        row_term(s, buf.at[s, 0], norms)
         each_piece(functools.partial(
-            lambda s, at: block(s, buf.at[s, 0], buf.at[s, 0], dbuf.at[s, 0], at, acc, None, False),
+            lambda s, at: block(s, buf.at[s, 0], buf.at[s, 0], dbuf.at[s, 0], at, acc, None, False,
+                                norms),
             s))
 
     for s in range(slots):
@@ -196,11 +201,22 @@
                     forward(1 - s, 0)[k].wait_send()
                 moves[k].start()
 
+    def end_piece(s, k):
+        if k == 0:
+            for copy in back(s):
+                copy.wait_recv()
+            row_term(s, buf.at[s, n - 1], norms_end)
+            ext_acc[s] = jnp.zeros(ext_acc.shape[1:], jnp.float32)
+        block(s, buf.at[s, n - 2], buf.at[s, n - 1], dbuf.at[s, n - 2], pieces[k], ext_acc.at[s],
+              (dbuf.at[s, n - 1], cout.at[s, n - 2]), True, norms_end)
+        for copy in give_last(s, k):
+            copy.start()
+
     def turn(d, _):
         for k, at in enumerate(pieces):
             for s in range(slots):
                 @pl.when(pos[s] >= d)
-                def _(s=s, k=k, at=at):
+                def _(s=s, k=k):
                     forward(s, d - 1)[k].wait_recv()
 
                     @pl.when((pos[s] < n - 1) & (d < n - 2))
@@ -214,31 +230,39 @@
                         def _():
                             forward(s, d)[-1].start()
 
+            for s in range(slots):
+                @pl.when(pos[s] >= d)
+                def _(s=s, k=k, at=at):
                     block(s, buf.at[s, d], buf.at[s, 0], dbuf.at[s, d], at, acc,
-                          (dbuf.at[s, 0], cout.at[s, d]), False)
-
-                    @pl.when((pos[s] != n - 2) | (d != n - 2))
+                          (dbuf.at[s, 0], cout.at[s, d]), False, norms)
+
+                    @pl.when(d < n - 2)
                     def _():
-                        for copy in give(s, d, k):
+                        give(s, d, k).start()
+
+                    @pl.when((pos[s] == n - 1) & (d == n - 2))
+                    def _():
+                        for copy in give_last(s, k):
                             copy.start()
+
+                    if k < len(pieces) - 1:
+                        @pl.when((pos[s] == n - 2) & (d == n - 2))
+                        def _():
+                            end_piece(s, k)
         return 0
 
     lax.fori_loop(1, n - 1, turn, 0)
 
-    for s in range(slots):
-        @pl.when(pos[s] == n - 2)
-        def _(s=s):
-            for copy in back(s):
-                copy.wait_recv()
-            row_term(s, buf.at[s, n - 1])
-            ext_acc[s] = jnp.zeros(ext_acc.shape[1:], jnp.float32)
-            for k, at in enumerate(pieces):
-                block(s, buf.at[s, n - 2], buf.at[s, n - 1], dbuf.at[s, n - 2], at, ext_acc.at[s],
-                      (dbuf.at[s, n - 1], cout.at[s, n - 2]), True)
-                for copy in give(s, n - 2, k):
-                    copy.start()
-            for copy in give_end(s):
-                copy.start()
+    def collect(d, _):
+        for s in range(slots):
+            @pl.when(pos[s] + d <= n - 1)
+            def _(s=s):
+                for k in range(len(pieces)):
+                    give(s, d, k).wait_recv()
+                acc[...] += cin[s, d]
+        return 0
+
+    lax.fori_loop(1, n - 2, collect, 0)
 
     part[0] = acc[0:8, :]
     part[1] = acc[8:16, :]
@@ -251,6 +275,14 @@
     for k in range(len(cross)):
         swap(k).start()
     gath[here] = part[c]
+
+    for s in range(slots):
+        @pl.when(pos[s] == n - 2)
+        def _(s=s):
+            end_piece(s, len(pieces) - 1)
+            for copy in give_end(s):
+                copy.start()
+
 
     def place(s, core):
         return pos[s] if slots == 2 else z * (1 - core) + (n - 1 - z) * core
@@ -264,27 +296,16 @@
         summed = summed + gath[k]
     tot[...] = summed
 
-    def collect(d, _):
-        for s in range(slots):
-            for core in range(2):
-                @pl.when(place(s, core) + d <= n - 1)
-                def _(s=s, core=core):
+    for s in range(slots):
+        for core in range(2):
+            for e in range(2):
+                @pl.when((place(s, core) <= 1) if e == 0 else (place(s, core) == n - 1))
+                def _(s=s, core=core, e=e):
                     for other in range(xs):
                         source = other * 2 + core
-                        for k in range(len(pieces)):
-                            taken(s, d, k, source).wait_recv()
-                        tot[...] += cin[s, d, source]
-        return 0
-
-    lax.fori_loop(1, n - 1, collect, 0)
-    for s in range(slots):
-        for core in range(2):
-            @pl.when(place(s, core) == n - 1)
-            def _(s=s, core=core):
-                for other in range(xs):
-                    source = other * 2 + core
-                    taken(s, None, 0, source).wait_recv()
-                    tot[...] += cin[s, n - 1, source]
+                        for k in range(1 if e else len(pieces)):
+                            taken(s, e, k, source).wait_recv()
+                        tot[...] += late[s, e, source]
     summed = tot[...]
     row = lax.broadcasted_iota(jnp.int32, (8, 1), 0)
     ridge = jnp.zeros((8, 1), jnp.float32)
@@ -347,8 +368,14 @@
             @pl.when(pos[s] >= d)
             def _(s=s):
                 for k in range(len(pieces)):
-                    for copy in give(s, d, k):
-                        copy.wait_send()
+                    @pl.when(d < n - 2)
+                    def _(k=k):
+                        give(s, d, k).wait_send()
+
+                    @pl.when(d == n - 2)
+                    def _(k=k):
+                        for copy in give_last(s, k):
+                            copy.wait_send()
 
                 @pl.when((pos[s] < n - 1) & (d < n - 2))
                 def _():
@@ -390,8 +417,10 @@
             pltpu.VMEM((2 * cols, rows), f32),
             pltpu.VMEM((slots, 2 * cols, rows), f32),
             pltpu.VMEM((slots, 8, rows), f32),
+            pltpu.VMEM((slots, 8, rows), f32),
             pltpu.VMEM((slots, n, 2 * cols, rows), f32),
-            pltpu.VMEM((slots, n, 2 * xs, cols, rows), f32),
+            pltpu.VMEM((slots, n, 2 * cols, rows), f32),
+            pltpu.VMEM((slots, 2, 2 * xs, cols, rows), f32),
             pltpu.VMEM((2, cols, rows), f32),
             pltpu.VMEM((2 * xs, cols, rows), f32),
             pltpu.VMEM((cols, rows), f32),
@@ -401,8 +430,8 @@
             dma((slots, n, chunks)), dma((slots, n, chunks)),
             dma((slots, n)), dma((slots, n)),
             dma, dma,
-            dma((slots, n, chunks, 2 * xs)), dma((slots, n, chunks, 2 * xs)),
-            dma((slots, 2 * xs)),
+            dma((slots, n, chunks)), dma((slots, n, chunks)),
+            dma((slots, 2, chunks, 2 * xs)), dma((slots, 2, chunks, 2 * xs)),
             dma((2 * xs - 1,)), dma((2 * xs - 1,)),
             dma((n,)), dma((n,)),
         ],

time: 42.2 us -> 36.9 us (0.87)
  Pallas kernels: 39.9 us -> 34.5 us
    pallas_call x1, Pallas kernels: 39.9 us -> 34.5 us  [per_device(): pl.pallas_call(functools.partial(cg_kernel, n, slots, tile), out_shape=(o...]
where the time goes in v4:
time: 36.9 us; the launch traced here: 36.7 us
  Pallas kernels  34.5 us (93%)
  other arithmetic  1.44 us (4%)
  between operations  0.69 us (2%)
    pallas_call x1, Pallas kernels, per_device(): pl.pallas_call(functools.partial(cg_kernel, n, slots, tile), out_shape=(o...  34.5 us
    add x1, other arithmetic, per_device(): direction_next = residual_next + ratio * direction  1.44 us

profile of v4, /device:TPU:0, one launch (start us, length us, event | category | flops | bytes accessed | tf_op | source)
XLA Modules:
  0.0 36.7 jit_solution(4152155765712362166)
XLA Ops:
  0.6 0.0 copy-start
  0.6 0.0 copy-start.1
  0.7 0.0 copy-start.2
  0.7 34.5 %shard_map.94 = (f32[8,1024]{1,0:T(8,128)}, f32[8,1024]{1,0:T(8,128)}, f32[8,1024]{1,0:T(8,128)}) custom-call(f32[8]{0:T(128)} %scale_hbm.1, f32[8]{0:T(128)} %weight_hbm.1, f32[8]{0:T(128)} %ridge_hbm.1, bf16[4,1024,128]{2,1,0:T(8,128)(2,1)} %feats_ref.1, f32[8,1024]{1,0:T(8,128)} %bitcast.18, f32[8,1024]{1,0:T(8,128)} %bitcast.17), custom_call_target="tpu_custom_call" | custom-call | tf_op jit(solution)/shard_map/pallas_call | solution.py:404
  35.2 0.0 copy-done
  35.2 0.0 copy-done.1
  35.2 0.0 copy-done.2
  35.2 1.4 %fusion = (f32[1024,8]{0,1:T(8,128)}, f32[1024,8]{0,1:T(8,128)}, f32[1024,8]{0,1:T(8,128)}) fusion(f32[1024,8]{0,1:T(8,128)S(1)} %copy-done, f32[8,1024]{1,0:T(8,128)} %get-tuple-element.8, f32[1024,8]{0,1:T(8,128)S(1)} %copy-done.1, f32[8,1024]{1,0:T(8,128)} %get-tuple-element.7, f32[8,1024]{1,0:T(8,128)} %get-tuple-element.6, f32[1024,8]{0,1:T(8,128)S(1)} %copy-done.2), kind=kLoop, calls=%fused_computation.1 | loop fusion | flops 49152 | bytes 294912 | tf_op jit(solution)/shard_map/add | solution.py:447
Async XLA Ops:
  0.6 34.6 %copy-start = (f32[1024,8]{0,1:T(8,128)S(1)}, f32[1024,8]{0,1:T(8,128)}, u32[]{:S(2)}) copy-start(f32[1024,8]{0,1:T(8,128)} %param.13) | copy-start | bytes 98308
  0.6 34.6 %copy-start.1 = (f32[1024,8]{0,1:T(8,128)S(1)}, f32[1024,8]{0,1:T(8,128)}, u32[]{:S(2)}) copy-start(f32[1024,8]{0,1:T(8,128)} %param.12) | copy-start | bytes 98308
  0.7 34.6 %copy-start.2 = (f32[1024,8]{0,1:T(8,128)S(1)}, f32[1024,8]{0,1:T(8,128)}, u32[]{:S(2)}) copy-start(f32[1024,8]{0,1:T(8,128)} %param.11) | copy-start | bytes 98308

commit v5 on v4

--- a/solution.py
+++ b/solution.py
@@ -66,6 +66,25 @@
         pl.semaphore_signal(
             barrier, inc=1, device_id_type=MESH,
             device_id={"views": lax.rem(x + dx, xs), "rhs": lax.rem(c + dc, 2)})
+
+    def consts(s):
+        index = first_view + view[s]
+        rate = scale_ref[index] * math.log2(math.e)
+        return rate, jnp.log2(jnp.full((1, 1), weight_ref[index], jnp.float32))
+
+    def row_term(s, slot_ref, norms):
+        rate, low_weight = consts(s)
+        feats = slot_ref[...].astype(jnp.float32)
+        sums = lax.dot_general(
+            jnp.ones((8, feats.shape[1]), jnp.float32), feats * feats, LANES,
+            precision=lax.Precision.HIGHEST, preferred_element_type=jnp.float32,
+        )
+        norms[s] = low_weight - rate * sums
+
+    for copy in fetch:
+        copy.wait()
+    for s in range(slots):
+        load(s).wait()
     pl.semaphore_wait(barrier, len(cross) + sides)
 
     def remote(src, dst, send, recv, target):
@@ -124,40 +143,23 @@
         return remote(cout.at[s, n - 2, pl.ds(0, 8), at], late.at[s, e, source, :, at],
                       ls.at[s, e, k, 0], lr.at[s, e, k, source], ahead(s, 1))
 
-    for copy in fetch:
-        copy.wait()
+    for s in range(slots):
+        @pl.when(pos[s] < n - 1)
+        def _(s=s):
+            forward(s, 0)[0].start()
+
     pair = remote(dpair.at[c], dpair.at[c], ps, pr, {"rhs": 1 - c})
     pair.start()
-    for s in range(slots):
-        load(s).wait()
+    pair.wait_recv()
+    low = jnp.concatenate([dpair[0], dpair[1]], axis=0).astype(jnp.bfloat16)
+    for s in range(slots):
+        dbuf[s, 0] = low
 
         @pl.when(pos[s] < n - 1)
         def _(s=s):
-            for copy in forward(s, 0)[:-1]:
+            forward(s, 0)[-1].start()
+            for copy in forward(s, 0)[1:-1]:
                 copy.start()
-
-    pair.wait()
-    low = jnp.concatenate([dpair[0], dpair[1]], axis=0).astype(jnp.bfloat16)
-    for s in range(slots):
-        dbuf[s, 0] = low
-
-        @pl.when(pos[s] < n - 1)
-        def _(s=s):
-            forward(s, 0)[-1].start()
-
-    def consts(s):
-        index = first_view + view[s]
-        rate = scale_ref[index] * math.log2(math.e)
-        return rate, jnp.log2(jnp.full((1, 1), weight_ref[index], jnp.float32))
-
-    def row_term(s, slot_ref, norms):
-        rate, low_weight = consts(s)
-        feats = slot_ref[...].astype(jnp.float32)
-        sums = lax.dot_general(
-            jnp.ones((8, feats.shape[1]), jnp.float32), feats * feats, LANES,
-            precision=lax.Precision.HIGHEST, preferred_element_type=jnp.float32,
-        )
-        norms[s] = low_weight - rate * sums
 
     def block(s, jb, ib, jd, at, i_sum, j_sum, add_j, norms):
         rate, _ = consts(s)
@@ -183,9 +185,10 @@
 
         lax.fori_loop(0, rows // tile, step, 0)
 
+    for s in range(slots):
+        row_term(s, buf.at[s, 0], norms)
     acc[...] = jnp.zeros_like(acc)
     for s in range(slots):
-        row_term(s, buf.at[s, 0], norms)
         each_piece(functools.partial(
             lambda s, at: block(s, buf.at[s, 0], buf.at[s, 0], dbuf.at[s, 0], at, acc, None, False,
                                 norms),
@@ -288,7 +291,7 @@
         return pos[s] if slots == 2 else z * (1 - core) + (n - 1 - z) * core
 
     for k in range(len(cross)):
-        swap(k).wait()
+        swap(k).wait_recv()
     direction = dpair[c]
     residual = res_ref[...]
     summed = gath[0]
@@ -330,7 +333,7 @@
     for k in range(1, n):
         spread(k).start()
     for k in range(1, n):
-        spread(k).wait()
+        spread(k).wait_recv()
     sums = stats[0]
     for k in range(1, n):
         sums = sums + stats[k]
@@ -340,6 +343,11 @@
     step_out[...] = jnp.broadcast_to(step_size, step_out.shape)
     ratio_out[...] = jnp.broadcast_to(norm_next / norm_now, ratio_out.shape)
 
+    pair.wait_send()
+    for k in range(len(cross)):
+        swap(k).wait_send()
+    for k in range(1, n):
+        spread(k).wait_send()
     for s in range(slots):
         @pl.when(pos[s] < n - 1)
         def _(s=s):

time: 36.9 us -> 36.4 us (0.986)
  Pallas kernels: 34.5 us -> 34.1 us
    pallas_call x1, Pallas kernels: 34.5 us -> 34.1 us  [per_device(): pl.pallas_call(functools.partial(cg_kernel, n, slots, tile), out_shape=(o...]
where the time goes in v5:
time: 36.4 us; the launch traced here: 36.2 us
  Pallas kernels  34.1 us (94%)
  other arithmetic  1.44 us (4%)
  between operations  0.69 us (2%)
    pallas_call x1, Pallas kernels, per_device(): pl.pallas_call(functools.partial(cg_kernel, n, slots, tile), out_shape=(o...  34.1 us
    add x1, other arithmetic, per_device(): direction_next = residual_next + ratio * direction  1.44 us

profile of v5, /device:TPU:0, one launch (start us, length us, event | category | flops | bytes accessed | tf_op | source)
XLA Modules:
  0.0 36.2 jit_solution(13925635971613420787)
XLA Ops:
  0.6 0.0 copy-start
  0.6 0.0 copy-start.1
  0.7 0.0 copy-start.2
  0.7 34.1 %shard_map.94 = (f32[8,1024]{1,0:T(8,128)}, f32[8,1024]{1,0:T(8,128)}, f32[8,1024]{1,0:T(8,128)}) custom-call(f32[8]{0:T(128)} %scale_hbm.1, f32[8]{0:T(128)} %weight_hbm.1, f32[8]{0:T(128)} %ridge_hbm.1, bf16[4,1024,128]{2,1,0:T(8,128)(2,1)} %feats_ref.1, f32[8,1024]{1,0:T(8,128)} %bitcast.18, f32[8,1024]{1,0:T(8,128)} %bitcast.17), custom_call_target="tpu_custom_call" | custom-call | tf_op jit(solution)/shard_map/pallas_call | solution.py:412
  34.7 0.0 copy-done
  34.7 0.0 copy-done.1
  34.8 0.0 copy-done.2
  34.8 1.4 %fusion = (f32[1024,8]{0,1:T(8,128)}, f32[1024,8]{0,1:T(8,128)}, f32[1024,8]{0,1:T(8,128)}) fusion(f32[1024,8]{0,1:T(8,128)S(1)} %copy-done, f32[8,1024]{1,0:T(8,128)} %get-tuple-element.8, f32[1024,8]{0,1:T(8,128)S(1)} %copy-done.1, f32[8,1024]{1,0:T(8,128)} %get-tuple-element.7, f32[8,1024]{1,0:T(8,128)} %get-tuple-element.6, f32[1024,8]{0,1:T(8,128)S(1)} %copy-done.2), kind=kLoop, calls=%fused_computation.1 | loop fusion | flops 49152 | bytes 294912 | tf_op jit(solution)/shard_map/add | solution.py:455
Async XLA Ops:
  0.6 34.1 %copy-start = (f32[1024,8]{0,1:T(8,128)S(1)}, f32[1024,8]{0,1:T(8,128)}, u32[]{:S(2)}) copy-start(f32[1024,8]{0,1:T(8,128)} %param.13) | copy-start | bytes 98308
  0.6 34.1 %copy-start.1 = (f32[1024,8]{0,1:T(8,128)S(1)}, f32[1024,8]{0,1:T(8,128)}, u32[]{:S(2)}) copy-start(f32[1024,8]{0,1:T(8,128)} %param.12) | copy-start | bytes 98308
  0.7 34.1 %copy-start.2 = (f32[1024,8]{0,1:T(8,128)S(1)}, f32[1024,8]{0,1:T(8,128)}, u32[]{:S(2)}) copy-start(f32[1024,8]{0,1:T(8,128)} %param.11) | copy-start | bytes 98308
